TPU v7x, 128 devices: a whole 4x4x4 slice. The times are simulated.
128 devices in a mesh: src: 16 (over z, y), tgt: 8 (over x, core).
Axes of the slice: x: 4, y: 4, z: 4, core: 2. Of those that a mesh axis runs over, the one named last changes fastest.
Arguments:
- src_points: float32 [64, 32768], P(None, ('src', 'tgt')), as said below
- tgt_points: float32 [64, 32768], P(None, ('tgt', 'src')), as said below
- log_a: float32 [32768], P('src'), may hold values from -1 to 1
- log_b: float32 [32768], P('tgt'), may hold values from -1 to 1
- g_init: float32 [32768], P('tgt')
Outputs:
- f_out: float32 [32768], P('src')
- g_out: float32 [32768], P('tgt')
- grad_src: float32 [64, 32768], P(None, ('src', 'tgt'))
- grad_tgt: float32 [64, 32768], P(None, ('tgt', 'src'))
Inputs may be any that keep to these rules, and one draw needn't show every extreme that they name: `src_points`: entries of order one or less. `tgt_points`: entries of order one or less.
All inputs are finite; a program needn't handle non-finite values.
Results may differ from a plain program's by a relative error of at most 0.0003.
Values sent between devices are 32-bit elements; how exact they have to be, the bound alone decides.
A program may use at most 64 MiB of HBM per device.

v0:
```python
import jax
import jax.numpy as jnp
from jax import lax
from jax.sharding import PartitionSpec as P

epsilon = 0.5
tile_rows = 512
highest = lax.Precision.HIGHEST


def per_device(src_points, tgt_points, log_a, log_b, g_init):
    sources = lax.all_gather(src_points, "tgt", axis=1, tiled=True)
    targets = lax.all_gather(tgt_points, "src", axis=1, tiled=True)
    width = sources.shape[0]
    num_rows = sources.shape[1]
    num_cols = targets.shape[1]
    row_block = min(tile_rows, num_rows)
    num_blocks = num_rows // row_block
    src_square = jnp.sum(sources * sources, axis=0)
    tgt_square = jnp.sum(targets * targets, axis=0)

    def tile_at(position):
        start = position * row_block
        src_part = lax.dynamic_slice_in_dim(sources, start, row_block, 1)
        src_norm = lax.dynamic_slice_in_dim(src_square, start, row_block, 0)
        cross = lax.dot_general(
            src_part,
            targets,
            (((0,), (0,)), ((), ())),
            precision=highest,
            preferred_element_type=jnp.float32,
        )
        return (start, src_part, src_norm[:, None] + tgt_square[None, :] - 2.0 * cross)

    def row_step(position, state):
        peaks, totals = state
        start, src_part, cost = tile_at(position)
        scores = (g_init[None, :] - cost) / epsilon
        peak = jnp.max(scores, axis=1)
        total = jnp.sum(jnp.exp(scores - peak[:, None]), axis=1)
        peaks = lax.dynamic_update_slice_in_dim(peaks, peak, start, 0)
        totals = lax.dynamic_update_slice_in_dim(totals, total, start, 0)
        return (peaks, totals)

    zero_rows = jnp.zeros((num_rows,), jnp.float32)
    row_peak, row_total = lax.fori_loop(0, num_blocks, row_step, (zero_rows, zero_rows))
    global_peak = lax.pmax(row_peak, "tgt")
    row_total = lax.psum(row_total * jnp.exp(row_peak - global_peak), "tgt")
    row_peak = global_peak
    f_out = epsilon * (log_a - (row_peak + jnp.log(row_total)))

    def column_step(position, state):
        peak, total, weighted = state
        start, src_part, cost = tile_at(position)
        row_part = lax.dynamic_slice_in_dim(f_out, start, row_block, 0)
        scores = (row_part[:, None] - cost) / epsilon
        top = jnp.maximum(peak, jnp.max(scores, axis=0))
        factor = jnp.exp(peak - top)
        expos = jnp.exp(scores - top[None, :])
        total = total * factor + jnp.sum(expos, axis=0)
        return (top, total, weighted)

    start_weighted = jnp.zeros((1, num_cols), jnp.float32)
    start_peak = jnp.full((num_cols,), -1e30, jnp.float32)
    start_total = jnp.zeros((num_cols,), jnp.float32)
    local_peak, local_total, weighted = lax.fori_loop(
        0, num_blocks, column_step, (start_peak, start_total, start_weighted)
    )
    col_peak = lax.pmax(local_peak, "src")
    col_total = lax.psum(local_total * jnp.exp(local_peak - col_peak), "src")
    g_out = epsilon * (log_b - (col_peak + jnp.log(col_total)))

    def gradient_step(position, state):
        src_grad, col_mass, pulled = state
        start, src_part, cost = tile_at(position)
        row_part = lax.dynamic_slice_in_dim(f_out, start, row_block, 0)
        plan = jnp.exp((row_part[:, None] + g_out[None, :] - cost) / epsilon)
        row_mass = jnp.sum(plan, axis=1)
        pushed = lax.dot_general(
            targets,
            plan,
            (((1,), (1,)), ((), ())),
            precision=highest,
            preferred_element_type=jnp.float32,
        )
        block_grad = 2.0 * (src_part * row_mass[None, :] - pushed)
        src_grad = lax.dynamic_update_slice_in_dim(src_grad, block_grad, start, 1)
        col_mass = col_mass + jnp.sum(plan, axis=0)
        pulled = pulled + jnp.dot(
            src_part, plan, precision=highest, preferred_element_type=jnp.float32
        )
        return (src_grad, col_mass, pulled)

    start_pulled = jnp.zeros((width, num_cols), jnp.float32)
    start_grad = jnp.zeros((width, num_rows), jnp.float32)
    src_grad, col_mass, pulled = lax.fori_loop(
        0, num_blocks, gradient_step, (start_grad, start_total, start_pulled)
    )
    grad_src = lax.psum_scatter(src_grad, "tgt", scatter_dimension=1, tiled=True)
    grad_tgt = lax.psum_scatter(
        2.0 * (targets * col_mass[None, :] - pulled), "src", scatter_dimension=1, tiled=True
    )
    return (f_out, g_out, grad_src, grad_tgt)


def solution(mesh):
    in_specs = (P(None, ("src", "tgt")), P(None, ("tgt", "src")), P("src"), P("tgt"), P("tgt"))
    out_specs = (P("src"), P("tgt"), P(None, ("src", "tgt")), P(None, ("tgt", "src")))
    return jax.shard_map(
        per_device, mesh=mesh, in_specs=in_specs, out_specs=out_specs, check_vma=False
    )
```

profile of v0, /device:TPU:1, one launch (start us, length us, event | category | flops | bytes accessed | tf_op | source)
XLA Modules:
  0.0 520.4 jit_solution(9644470165209914341)
XLA Ops:
  7.2 0.7 all-gather.2.cloned.1.call-update
  8.0 15.0 %all_gather.6 = f32[64,2048]{1,0:T(8,128)S(1)} all-gather(f32[64,256]{1,0:T(8,128)} %param.11), channel_id=1, replica_groups=mesh['src'=16,'tgt'=8] {'tgt'}, dimensions={1}, use_global_device_ids=true | all-gather | bytes 589824 | tf_op jit(solution)/shard_map/all_gather | solution.py:12
  23.0 32.4 %all-gather.2.cloned.1.call-done = f32[64,4096]{1,0:T(8,128)} async-done(((f32[64,256]{1,0:T(8,128)}), f32[64,4096]{1,0:T(8,128)}) %all-gather.2.cloned.1.call-update) | async-done | bytes 1048592 | tf_op jit(solution)/shard_map/all_gather | solution.py:13
  55.5 1.3 multiply_reduce_fusion
  56.8 45.5 %while.49 = (s32[]{:T(128)}, f32[2048]{0:T(1024)S(1)}, f32[2048]{0:T(1024)S(1)}, f32[4096]{0:T(1024)}, f32[2048]{0:T(1024)S(1)}, /*index=5*/f32[4096]{0:T(1024)S...) while((s32[]{:T(128)}, f32[2048]{0:T(1024)S(1)}, ...), condition=%wide.region_5.0_spmd, body=%wide.region_2.0_spmd.sunk | while | flops 1627388928 | bytes 18010292 | solution.py:46
  56.9 0.1 dynamic_slice.88
  56.9 9.5 %fusion.34 = (f32[512]{0:T(512)S(1)}, f32[512,4096]{1,0:T(8,128)S(1)}) fusion(f32[64,4096]{1,0:T(8,128)} %get-tuple-element.785, f32[64,2048]{1,0:T(8,128)S(1)} %get-tuple-element.784, s32[]{:T(128)S(6)} %select_n.34, f32[4096]{0:T(1024)S(1)} %get-tuple-element.783, f32[512]{0:T(512)S(1)} %dynamic_slice.88, f32[4096]{0:T(1024)} %get-tuple-element.781), kind=kOutput, calls=%fused_computation.30.clone.1 | convolution fusion | flops 1623195136 | bytes 9605124 | tf_op jit(solution)/shard_map/while/body/eval_jaxpr/dot_general | solution.py:26
  66.5 1.3 exponential_reduce_fusion.4
  67.7 0.3 dynamic_update_slice.26
  68.0 0.3 dynamic_update_slice.27
  68.3 9.5 %fusion.34 = (f32[512]{0:T(512)S(1)}, f32[512,4096]{1,0:T(8,128)S(1)}) fusion(f32[64,4096]{1,0:T(8,128)} %get-tuple-element.785, f32[64,2048]{1,0:T(8,128)S(1)} %get-tuple-element.784, s32[]{:T(128)S(6)} %select_n.34, f32[4096]{0:T(1024)S(1)} %get-tuple-element.783, f32[512]{0:T(512)S(1)} %dynamic_slice.88, f32[4096]{0:T(1024)} %get-tuple-element.781), kind=kOutput, calls=%fused_computation.30.clone.1 | convolution fusion | flops 1623195136 | bytes 9605124 | tf_op jit(solution)/shard_map/while/body/eval_jaxpr/dot_general | solution.py:26
  77.9 1.3 exponential_reduce_fusion.4
  79.1 0.3 dynamic_update_slice.26
  79.4 0.3 dynamic_update_slice.27
  79.7 0.1 dynamic_slice.88
  79.7 9.5 %fusion.34 = (f32[512]{0:T(512)S(1)}, f32[512,4096]{1,0:T(8,128)S(1)}) fusion(f32[64,4096]{1,0:T(8,128)} %get-tuple-element.785, f32[64,2048]{1,0:T(8,128)S(1)} %get-tuple-element.784, s32[]{:T(128)S(6)} %select_n.34, f32[4096]{0:T(1024)S(1)} %get-tuple-element.783, f32[512]{0:T(512)S(1)} %dynamic_slice.88, f32[4096]{0:T(1024)} %get-tuple-element.781), kind=kOutput, calls=%fused_computation.30.clone.1 | convolution fusion | flops 1623195136 | bytes 9605124 | tf_op jit(solution)/shard_map/while/body/eval_jaxpr/dot_general | solution.py:26
  89.3 1.3 exponential_reduce_fusion.4
  90.5 0.3 dynamic_update_slice.26
  90.8 0.2 dynamic_update_slice.27
  91.0 0.1 dynamic_slice.88
  91.1 9.5 %fusion.34 = (f32[512]{0:T(512)S(1)}, f32[512,4096]{1,0:T(8,128)S(1)}) fusion(f32[64,4096]{1,0:T(8,128)} %get-tuple-element.785, f32[64,2048]{1,0:T(8,128)S(1)} %get-tuple-element.784, s32[]{:T(128)S(6)} %select_n.34, f32[4096]{0:T(1024)S(1)} %get-tuple-element.783, f32[512]{0:T(512)S(1)} %dynamic_slice.88, f32[4096]{0:T(1024)} %get-tuple-element.781), kind=kOutput, calls=%fused_computation.30.clone.1 | convolution fusion | flops 1623195136 | bytes 9605124 | tf_op jit(solution)/shard_map/while/body/eval_jaxpr/dot_general | solution.py:26
  100.6 1.3 exponential_reduce_fusion.4
  101.9 0.3 dynamic_update_slice.26
  102.1 0.2 dynamic_update_slice.27
  102.3 14.0 %pmax.14 = f32[2048]{0:T(1024)S(1)} all-reduce(f32[2048]{0:T(1024)S(1)} %get-tuple-element.455), channel_id=1, replica_groups=mesh['src'=16,'tgt'=8] {'tgt'}, use_global_device_ids=true, to_apply=%region_6.0 | all-reduce | flops 2048 | bytes 16384 | tf_op jit(solution)/shard_map/pmax | solution.py:47
  116.4 13.6 %psum.14 = f32[2048]{0:T(1024)S(1)} all-reduce(f32[2048]{0:T(1024)S(1)} %exponential_multiply_fusion.1), channel_id=1, replica_groups=mesh['src'=16,'tgt'=8] {'tgt'}, use_global_device_ids=true, to_apply=%region_7.0 | all-reduce | flops 2048 | bytes 16384 | tf_op jit(solution)/shard_map/psum | solution.py:48
  130.0 43.7 %while.50 = (s32[]{:T(128)}, f32[4096]{0:T(1024)S(1)}, f32[4096]{0:T(1024)S(1)}, f32[2048]{0:T(1024)S(1)}, f32[2048]{0:T(1024)S(1)}, /*index=5*/f32[4096]{0:T(10...) while((s32[]{:T(128)}, f32[4096]{0:T(1024)S(1)}, ...), condition=%wide.region_11.0_spmd.clone, body=%wide.region_8.0_spmd.clone.sunk | while | flops 1627410432 | bytes 18198720 | solution.py:66
  130.0 0.1 dynamic_slice.90
  130.1 0.1 dynamic_slice.91
  130.2 9.4 %fusion.36 = (f32[4096]{0:T(1024)S(1)}, f32[512,4096]{1,0:T(8,128)S(1)}) fusion(f32[64,4096]{1,0:T(8,128)} %get-tuple-element.821, f32[64,2048]{1,0:T(8,128)S(1)} %get-tuple-element.820, s32[]{:T(128)S(6)} %select_n.35, f32[4096]{0:T(1024)S(1)} %get-tuple-element.819, f32[512]{0:T(512)S(1)} %dynamic_slice.90, f32[512]{0:T(512)S(1)} %dynamic_slice.91), kind=kOutput, calls=%fused_computation.31.clone.1 | convolution fusion | flops 1623191552 | bytes 9605124 | tf_op jit(solution)/shard_map/while/body/eval_jaxpr/dot_general | solution.py:26
  139.6 1.3 exponential_reduce_fusion.5
  141.0 0.1 dynamic_slice.90
  141.1 9.4 %fusion.36 = (f32[4096]{0:T(1024)S(1)}, f32[512,4096]{1,0:T(8,128)S(1)}) fusion(f32[64,4096]{1,0:T(8,128)} %get-tuple-element.821, f32[64,2048]{1,0:T(8,128)S(1)} %get-tuple-element.820, s32[]{:T(128)S(6)} %select_n.35, f32[4096]{0:T(1024)S(1)} %get-tuple-element.819, f32[512]{0:T(512)S(1)} %dynamic_slice.90, f32[512]{0:T(512)S(1)} %dynamic_slice.91), kind=kOutput, calls=%fused_computation.31.clone.1 | convolution fusion | flops 1623191552 | bytes 9605124 | tf_op jit(solution)/shard_map/while/body/eval_jaxpr/dot_general | solution.py:26
  150.5 1.3 exponential_reduce_fusion.5
  151.9 0.1 dynamic_slice.90
  152.0 0.1 dynamic_slice.91
  152.0 9.4 %fusion.36 = (f32[4096]{0:T(1024)S(1)}, f32[512,4096]{1,0:T(8,128)S(1)}) fusion(f32[64,4096]{1,0:T(8,128)} %get-tuple-element.821, f32[64,2048]{1,0:T(8,128)S(1)} %get-tuple-element.820, s32[]{:T(128)S(6)} %select_n.35, f32[4096]{0:T(1024)S(1)} %get-tuple-element.819, f32[512]{0:T(512)S(1)} %dynamic_slice.90, f32[512]{0:T(512)S(1)} %dynamic_slice.91), kind=kOutput, calls=%fused_computation.31.clone.1 | convolution fusion | flops 1623191552 | bytes 9605124 | tf_op jit(solution)/shard_map/while/body/eval_jaxpr/dot_general | solution.py:26
  161.4 1.3 exponential_reduce_fusion.5
  162.8 0.1 dynamic_slice.90
  163.0 9.4 %fusion.36 = (f32[4096]{0:T(1024)S(1)}, f32[512,4096]{1,0:T(8,128)S(1)}) fusion(f32[64,4096]{1,0:T(8,128)} %get-tuple-element.821, f32[64,2048]{1,0:T(8,128)S(1)} %get-tuple-element.820, s32[]{:T(128)S(6)} %select_n.35, f32[4096]{0:T(1024)S(1)} %get-tuple-element.819, f32[512]{0:T(512)S(1)} %dynamic_slice.90, f32[512]{0:T(512)S(1)} %dynamic_slice.91), kind=kOutput, calls=%fused_computation.31.clone.1 | convolution fusion | flops 1623191552 | bytes 9605124 | tf_op jit(solution)/shard_map/while/body/eval_jaxpr/dot_general | solution.py:26
  172.4 1.3 exponential_reduce_fusion.5
  173.7 57.9 %pmax.15 = f32[4096]{0:T(1024)S(1)} all-reduce(f32[4096]{0:T(1024)S(1)} %get-tuple-element.457), channel_id=1, replica_groups=mesh['src'=16,'tgt'=8] {'src'}, use_global_device_ids=true, to_apply=%region_12.0 | all-reduce | flops 4096 | bytes 32768 | tf_op jit(solution)/shard_map/pmax | solution.py:69
  231.7 55.9 %psum.15 = f32[4096]{0:T(1024)S(1)} all-reduce(f32[4096]{0:T(1024)S(1)} %exponential_multiply_fusion), channel_id=1, replica_groups=mesh['src'=16,'tgt'=8] {'src'}, use_global_device_ids=true, to_apply=%region_13.0 | all-reduce | flops 4096 | bytes 32768 | tf_op jit(solution)/shard_map/psum | solution.py:70
  287.6 98.3 %while.51 = (s32[]{:T(128)}, f32[64,2048]{1,0:T(8,128)S(1)}, f32[4096]{0:T(1024)S(1)}, f32[64,4096]{1,0:T(8,128)S(1)}, f32[64,2048]{1,0:T(8,128)S(1)}, /*index=5...) while((s32[]{:T(128)}, f32[64,2048]{1,0:T(8,128)S(1)}, ...), condition=%wide.region_17.0_spmd.clone, body=%wide.region_14.0_spmd.clone.sunk | while | flops 4849241600 | bytes 34193652 | solution.py:96
  287.8 0.1 dynamic_slice.95
  288.0 10.7 %fusion.43 = (f32[4096]{0:T(1024)S(1)}, f32[512]{0:T(512)S(1)}, f32[512,4096]{1,0:T(8,128)S(1)}) fusion(f32[64,4096]{1,0:T(8,128)} %get-tuple-element.863, f32[64,2048]{1,0:T(8,128)S(1)} %get-tuple-element.858, s32[]{:T(128)S(6)} %select_n.36, f32[4096]{0:T(1024)S(1)} %get-tuple-element.862, f32[512]{0:T(512)S(1)} %dynamic_slice.95, ...), kind=kOutput, calls=%fused_computation.29.clone.1 | convolution fusion | flops 1627385344 | bytes 9623556 | tf_op jit(solution)/shard_map/while/body/eval_jaxpr/dot_general | solution.py:26
  298.7 8.2 %fusion.44 = f32[64,2048]{1,0:T(8,128)S(1)} fusion(f32[64,2048]{1,0:T(8,128)S(1)} %get-tuple-element.841, s32[]{:T(128)S(6)} %select_n.36, f32[512,4096]{1,0:T(8,128)S(1)} %get-tuple-element.751, f32[64,4096]{1,0:T(8,128)S(1)} %copy-done, f32[64,2048]{1,0:T(8,128)S(1)} %get-tuple-element.858, f32[512]{0:T(512)S(1)} %get-tuple-element.752), kind=kOutput, calls=%fused_computation.16.clone.1 | convolution fusion | flops 1610711040 | bytes 9701380 | tf_op jit(solution)/shard_map/while/body/eval_jaxpr/dot_general | solution.py:79
  307.0 5.3 %convolution_add_fusion.2 = f32[64,4096]{1,0:T(8,128)S(1)} fusion(f32[512,4096]{1,0:T(8,128)S(1)} %get-tuple-element.751, f32[64,4096]{1,0:T(8,128)S(1)} %get-tuple-element.843, pred[]{:T(512)S(6)} %compare.7, f32[64,2048]{1,0:T(8,128)S(1)} %get-tuple-element.858, s32[]{:T(128)S(6)} %select_n.36), kind=kOutput, calls=%fused_computation.12.clone.1 | convolution fusion | flops 1611137024 | bytes 10616837 | tf_op jit(solution)/shard_map/while/body/eval_jaxpr/dot_general | solution.py:89
  312.3 0.1 dynamic_slice.95
  312.5 10.7 %fusion.43 = (f32[4096]{0:T(1024)S(1)}, f32[512]{0:T(512)S(1)}, f32[512,4096]{1,0:T(8,128)S(1)}) fusion(f32[64,4096]{1,0:T(8,128)} %get-tuple-element.863, f32[64,2048]{1,0:T(8,128)S(1)} %get-tuple-element.858, s32[]{:T(128)S(6)} %select_n.36, f32[4096]{0:T(1024)S(1)} %get-tuple-element.862, f32[512]{0:T(512)S(1)} %dynamic_slice.95, ...), kind=kOutput, calls=%fused_computation.29.clone.1 | convolution fusion | flops 1627385344 | bytes 9623556 | tf_op jit(solution)/shard_map/while/body/eval_jaxpr/dot_general | solution.py:26
  323.2 8.2 %fusion.44 = f32[64,2048]{1,0:T(8,128)S(1)} fusion(f32[64,2048]{1,0:T(8,128)S(1)} %get-tuple-element.841, s32[]{:T(128)S(6)} %select_n.36, f32[512,4096]{1,0:T(8,128)S(1)} %get-tuple-element.751, f32[64,4096]{1,0:T(8,128)S(1)} %copy-done, f32[64,2048]{1,0:T(8,128)S(1)} %get-tuple-element.858, f32[512]{0:T(512)S(1)} %get-tuple-element.752), kind=kOutput, calls=%fused_computation.16.clone.1 | convolution fusion | flops 1610711040 | bytes 9701380 | tf_op jit(solution)/shard_map/while/body/eval_jaxpr/dot_general | solution.py:79
  331.5 5.3 %convolution_add_fusion.2 = f32[64,4096]{1,0:T(8,128)S(1)} fusion(f32[512,4096]{1,0:T(8,128)S(1)} %get-tuple-element.751, f32[64,4096]{1,0:T(8,128)S(1)} %get-tuple-element.843, pred[]{:T(512)S(6)} %compare.7, f32[64,2048]{1,0:T(8,128)S(1)} %get-tuple-element.858, s32[]{:T(128)S(6)} %select_n.36), kind=kOutput, calls=%fused_computation.12.clone.1 | convolution fusion | flops 1611137024 | bytes 10616837 | tf_op jit(solution)/shard_map/while/body/eval_jaxpr/dot_general | solution.py:89
  336.8 0.1 dynamic_slice.95
  337.0 10.7 %fusion.43 = (f32[4096]{0:T(1024)S(1)}, f32[512]{0:T(512)S(1)}, f32[512,4096]{1,0:T(8,128)S(1)}) fusion(f32[64,4096]{1,0:T(8,128)} %get-tuple-element.863, f32[64,2048]{1,0:T(8,128)S(1)} %get-tuple-element.858, s32[]{:T(128)S(6)} %select_n.36, f32[4096]{0:T(1024)S(1)} %get-tuple-element.862, f32[512]{0:T(512)S(1)} %dynamic_slice.95, ...), kind=kOutput, calls=%fused_computation.29.clone.1 | convolution fusion | flops 1627385344 | bytes 9623556 | tf_op jit(solution)/shard_map/while/body/eval_jaxpr/dot_general | solution.py:26
  347.7 8.2 %fusion.44 = f32[64,2048]{1,0:T(8,128)S(1)} fusion(f32[64,2048]{1,0:T(8,128)S(1)} %get-tuple-element.841, s32[]{:T(128)S(6)} %select_n.36, f32[512,4096]{1,0:T(8,128)S(1)} %get-tuple-element.751, f32[64,4096]{1,0:T(8,128)S(1)} %copy-done, f32[64,2048]{1,0:T(8,128)S(1)} %get-tuple-element.858, f32[512]{0:T(512)S(1)} %get-tuple-element.752), kind=kOutput, calls=%fused_computation.16.clone.1 | convolution fusion | flops 1610711040 | bytes 9701380 | tf_op jit(solution)/shard_map/while/body/eval_jaxpr/dot_general | solution.py:79
  356.0 5.3 %convolution_add_fusion.2 = f32[64,4096]{1,0:T(8,128)S(1)} fusion(f32[512,4096]{1,0:T(8,128)S(1)} %get-tuple-element.751, f32[64,4096]{1,0:T(8,128)S(1)} %get-tuple-element.843, pred[]{:T(512)S(6)} %compare.7, f32[64,2048]{1,0:T(8,128)S(1)} %get-tuple-element.858, s32[]{:T(128)S(6)} %select_n.36), kind=kOutput, calls=%fused_computation.12.clone.1 | convolution fusion | flops 1611137024 | bytes 10616837 | tf_op jit(solution)/shard_map/while/body/eval_jaxpr/dot_general | solution.py:89
  361.4 0.1 dynamic_slice.95
  361.5 10.7 %fusion.43 = (f32[4096]{0:T(1024)S(1)}, f32[512]{0:T(512)S(1)}, f32[512,4096]{1,0:T(8,128)S(1)}) fusion(f32[64,4096]{1,0:T(8,128)} %get-tuple-element.863, f32[64,2048]{1,0:T(8,128)S(1)} %get-tuple-element.858, s32[]{:T(128)S(6)} %select_n.36, f32[4096]{0:T(1024)S(1)} %get-tuple-element.862, f32[512]{0:T(512)S(1)} %dynamic_slice.95, ...), kind=kOutput, calls=%fused_computation.29.clone.1 | convolution fusion | flops 1627385344 | bytes 9623556 | tf_op jit(solution)/shard_map/while/body/eval_jaxpr/dot_general | solution.py:26
  372.3 8.2 %fusion.44 = f32[64,2048]{1,0:T(8,128)S(1)} fusion(f32[64,2048]{1,0:T(8,128)S(1)} %get-tuple-element.841, s32[]{:T(128)S(6)} %select_n.36, f32[512,4096]{1,0:T(8,128)S(1)} %get-tuple-element.751, f32[64,4096]{1,0:T(8,128)S(1)} %copy-done, f32[64,2048]{1,0:T(8,128)S(1)} %get-tuple-element.858, f32[512]{0:T(512)S(1)} %get-tuple-element.752), kind=kOutput, calls=%fused_computation.16.clone.1 | convolution fusion | flops 1610711040 | bytes 9701380 | tf_op jit(solution)/shard_map/while/body/eval_jaxpr/dot_general | solution.py:79
  380.5 5.3 %convolution_add_fusion.2 = f32[64,4096]{1,0:T(8,128)S(1)} fusion(f32[512,4096]{1,0:T(8,128)S(1)} %get-tuple-element.751, f32[64,4096]{1,0:T(8,128)S(1)} %get-tuple-element.843, pred[]{:T(512)S(6)} %compare.7, f32[64,2048]{1,0:T(8,128)S(1)} %get-tuple-element.858, s32[]{:T(128)S(6)} %select_n.36), kind=kOutput, calls=%fused_computation.12.clone.1 | convolution fusion | flops 1611137024 | bytes 10616837 | tf_op jit(solution)/shard_map/while/body/eval_jaxpr/dot_general | solution.py:89
  385.9 0.8 copy-done.1
  386.7 2.4 subtract_multiply_fusion.2
  389.1 47.1 %reduce-scatter.3.cloned.1.call-done = f32[64,256]{1,0:T(8,128)} async-done(((f32[64,2048]{1,0:T(8,128)}), f32[64,256]{1,0:T(8,128)}) %reduce-scatter.3.cloned.1.call-update) | async-done | bytes 65552 | tf_op jit(solution)/shard_map/reduce_scatter | solution.py:99
  436.3 77.2 %reduce-scatter.5.cloned.1.call-done = f32[64,256]{1,0:T(8,128)} async-done(((f32[64,4096]{1,0:T(8,128)}), f32[64,256]{1,0:T(8,128)}) %reduce-scatter.5.cloned.1.call-update) | async-done | bytes 65552 | tf_op jit(solution)/shard_map/reduce_scatter | solution.py:100
  (57 shorter events, 1.0 us)
Async XLA Ops:
  7.2 48.3 %all-gather.2.cloned.1.call-start = ((), (), s32[]{:S(2)}) async-start(), calls=%async_computation.2 | async-start | bytes 1114112 | tf_op jit(solution)/shard_map/all_gather | solution.py:13
  7.9 428.4 %reduce-scatter.3.cloned.1.call-start = ((), (), s32[]{:S(2)}) async-start(), calls=%async_computation.3 | async-start | bytes 589824 | tf_op jit(solution)/shard_map/reduce_scatter | solution.py:99
  56.8 73.1 %copy-start.5 = (f32[2048]{0:T(1024)S(1)}, f32[2048]{0:T(1024)}, u32[]{:S(2)}) copy-start(f32[2048]{0:T(1024)} %param.13) | copy-start | bytes 24580
  130.0 157.5 %copy-start.3 = (f32[4096]{0:T(1024)S(1)}, f32[4096]{0:T(1024)}, u32[]{:S(2)}) copy-start(f32[4096]{0:T(1024)} %param.14) | copy-start | bytes 49156
  288.0 10.7 %copy-start = (f32[64,4096]{1,0:T(8,128)S(1)}, f32[64,4096]{1,0:T(8,128)}, u32[]{:S(2)}) copy-start(f32[64,4096]{1,0:T(8,128)} %get-tuple-element.863) | copy-start | bytes 3145732 | tf_op jit(solution)/shard_map/while
  312.5 10.7 %copy-start = (f32[64,4096]{1,0:T(8,128)S(1)}, f32[64,4096]{1,0:T(8,128)}, u32[]{:S(2)}) copy-start(f32[64,4096]{1,0:T(8,128)} %get-tuple-element.863) | copy-start | bytes 3145732 | tf_op jit(solution)/shard_map/while
  337.0 10.7 %copy-start = (f32[64,4096]{1,0:T(8,128)S(1)}, f32[64,4096]{1,0:T(8,128)}, u32[]{:S(2)}) copy-start(f32[64,4096]{1,0:T(8,128)} %get-tuple-element.863) | copy-start | bytes 3145732 | tf_op jit(solution)/shard_map/while
  361.5 10.7 %copy-start = (f32[64,4096]{1,0:T(8,128)S(1)}, f32[64,4096]{1,0:T(8,128)}, u32[]{:S(2)}) copy-start(f32[64,4096]{1,0:T(8,128)} %get-tuple-element.863) | copy-start | bytes 3145732 | tf_op jit(solution)/shard_map/while
  385.9 0.8 copy-start.1
  385.9 127.6 %copy-start.2 = (f32[2048]{0:T(1024)}, f32[2048]{0:T(1024)S(1)}, u32[]{:S(2)}) copy-start(f32[2048]{0:T(1024)S(1)} %get-tuple-element.884) | copy-start | bytes 24580
  385.9 127.6 %copy-start.4 = (f32[4096]{0:T(1024)}, f32[4096]{0:T(1024)S(1)}, u32[]{:S(2)}) copy-start(f32[4096]{0:T(1024)S(1)} %get-tuple-element.889) | copy-start | bytes 49156
  386.7 126.8 %reduce-scatter.5.cloned.1.call-start = ((), (), s32[]{:S(2)}) async-start(), calls=%async_computation.4 | async-start | bytes 1114112 | tf_op jit(solution)/shard_map/reduce_scatter | solution.py:100
Sparse Core Ops, SparseCore 0:
  10.1 45.3 all-gather.1
  386.8 49.4 reduce-scatter.2
  440.4 73.0 reduce-scatter.4
where the time goes:
time: 530 us; the launch traced here: 520 us
  matrix products  173 us (33%)
  waiting for transfers between devices  158 us (30%)
  blocking collectives  156 us (29%)
  other arithmetic  14.3 us (3%)
  between operations  14.3 us (3%)
    dot_general x12, matrix products, tile_at(): lax.dot_general(src_part, targets, (((0,), (0,)), ((), ())), precision=hi...  118 us
    reduce_scatter x1, waiting for transfers between devices, per_device(): lax.psum_scatter(2.0 * (targets * col_mass[None, :] - pulled), 'src', sca...  77.2 us
    pmax x1, blocking collectives, per_device(): col_peak = lax.pmax(local_peak, 'src')  57.9 us
    psum x1, blocking collectives, per_device(): col_total = lax.psum(local_total * jnp.exp(local_peak - col_peak), 'src')  55.9 us
    reduce_scatter x1, waiting for transfers between devices, per_device(): lax.psum_scatter(src_grad, 'tgt', scatter_dimension=1, tiled=True)  47.1 us
    dot_general x4, matrix products, gradient_step(): lax.dot_general(targets, plan, (((1,), (1,)), ((), ())), precision=highes...  33 us
    all_gather x1, waiting for transfers between devices, per_device(): targets = lax.all_gather(tgt_points, 'src', axis=1, tiled=True)  32.4 us
    dot_general x4, matrix products, gradient_step(): jnp.dot(src_part, plan, precision=highest, preferred_element_type=jnp.flo...  21.4 us
  transfers between devices with their start and end apart: 3, of which 3 were waited for; matrix products, arithmetic and copies ran while one was open for 0% of the time, Pallas kernels for 0%

commit v1 on v0

v1 whole, which is shorter than its diff:
```python
import functools

import jax
import jax.numpy as jnp
from jax import lax
from jax.experimental import pallas as pl
from jax.experimental.pallas import tpu as pltpu
from jax.sharding import PartitionSpec as P

epsilon = 0.5
LOG2E = 1.4426950408889634
LN2 = 0.6931471805599453
SCALE = LOG2E / epsilon
LO_SCALE = 2.0**17
PT_SCALE = 2.0**4
F8_MAX = 448.0
MESH = pl.DeviceIdType.MESH
f32, bf16, f8 = jnp.float32, jnp.bfloat16, jnp.float8_e4m3fn
LANES = 128


def split(value):
    high = value.astype(bf16).astype(f32)
    return high, value - high


def to_f8(value):
    return jnp.clip(value, -F8_MAX, F8_MAX).astype(f8)


def wide(column, times):
    return jnp.concatenate([column] * times, axis=1)


def kernel(
    ns, ny, nt, nc, comm,
    src_ref, tgt_ref, la_ref, lb_ref, g_ref,
    f_ref, go_ref, gs_ref, gt_ref,
    xall, yslots, xs, yt, w, w8, bcol, sbuf, mrun, lrun, arow, mcol, rowstat, colstat, srow,
    ehi, elo, pulled, left, left8, gsend, gsrecv, gtrecv,
    sx, rx, sy, ry, sr, rr, sc, rc, sgs, rgs, sgt, rgt,
):
    blk = src_ref.shape[1]
    width = src_ref.shape[0]
    rows, cols = nt * blk, ns * blk
    if comm:
        p, q = lax.axis_index("src"), lax.axis_index("tgt")
    else:
        p, q = jnp.int32(0), jnp.int32(0)

    def shifted(at, step, count, minor, sign):
        major = count // minor
        a = lax.rem(at // minor + sign * (step // minor) + major, major)
        b = lax.rem(lax.rem(at, minor) + sign * lax.rem(step, minor) + minor, minor)
        return a * minor + b

    def src_peer(step, sign):
        return shifted(p, jnp.int32(step), ns, ny, sign)

    def tgt_peer(step, sign):
        return shifted(q, jnp.int32(step), nt, nc, sign)

    def lanes(owner):
        return pl.ds(pl.multiple_of(owner * blk, blk), blk)

    def remote(source, target, send, recv, device):
        return pltpu.make_async_remote_copy(
            src_ref=source, dst_ref=target, send_sem=send, recv_sem=recv, device_id=device, device_id_type=MESH
        )

    tsteps = range(1, nt) if comm else ()
    ssteps = range(1, ns) if comm else ()

    def x_copy(k, owner, to):
        return remote(src_ref, xall.at[:, lanes(owner)], sx.at[k], rx.at[k], (p, to))

    def y_copy(k):
        return remote(tgt_ref, yslots.at[k], sy.at[k], ry.at[k], (src_peer(k, 1), q))

    def r_copy(k, owner, to):
        return remote(rowstat.at[q], rowstat.at[owner], sr.at[k], rr.at[k], (p, to))

    def c_copy(k, owner, to):
        return remote(colstat.at[p], colstat.at[owner], sc.at[k], rc.at[k], (to, q))

    def gs_copy(k):
        return remote(gsend.at[k], gsrecv.at[k], sgs.at[k], rgs.at[k], (p, tgt_peer(k, -1)))

    def gt_copy(k):
        return remote(pulled.at[k], gtrecv.at[k], sgt.at[k], rgt.at[k], (src_peer(k, -1), q))

    if comm:
        barrier = pltpu.get_barrier_semaphore()
        for k in tsteps:
            pl.semaphore_signal(barrier, inc=1, device_id=(p, tgt_peer(k, 1)), device_id_type=MESH)
        for k in ssteps:
            pl.semaphore_signal(barrier, inc=1, device_id=(src_peer(k, 1), q), device_id_type=MESH)
        pl.semaphore_wait(barrier, nt - 1 + ns - 1)

    for k in tsteps:
        x_copy(k, q, tgt_peer(k, 1)).start()
    for k in ssteps:
        y_copy(k).start()
    xall[:, lanes(q)] = src_ref[...]
    yslots[0] = tgt_ref[...]

    def prepare_targets(k, slot):
        y = yslots[k]
        scaled = y * (2.0 * SCALE)
        parts = jnp.concatenate(split(scaled), axis=0).T.astype(bf16)
        at = pl.ds(pl.multiple_of(k * blk, blk), blk)
        yt[at, 0:LANES] = parts
        yt[at, LANES : 2 * LANES] = parts
        bias = SCALE * (g_ref[:, lanes(src_peer(k, -1))] - jnp.sum(y * y, axis=0, keepdims=True))
        bcol[slot] = jnp.broadcast_to(bias, (LANES, blk)).T

    def prepare_sources(j):
        at = pl.ds(j * blk, blk)
        x = xall[:, at]
        high, low = split(x)
        xs[0:width, at] = high.astype(bf16)
        xs[width : 2 * width, at] = high.astype(bf16)
        xs[2 * width : 3 * width, at] = low.astype(bf16)
        xs[3 * width : 4 * width, at] = low.astype(bf16)
        w[at, 0:LANES] = jnp.concatenate([high, low], axis=0).T.astype(bf16)
        w[at, LANES : 2 * LANES] = jnp.ones((blk, LANES), bf16)
        parts = jnp.concatenate([x * PT_SCALE, jnp.ones_like(x)], axis=0).T
        w8[at, :] = to_f8(parts)

    def scores(k, slot):
        at = pl.ds(pl.multiple_of(k * blk, blk), blk)
        sbuf[slot] = jnp.dot(yt[at, :], xs[...], preferred_element_type=f32)

    def wait_y(k):
        if comm:
            y_copy(k).wait_recv()

    prepare_targets(0, 0)
    for k in tsteps:
        x_copy(k, tgt_peer(k, -1), tgt_peer(k, 1)).wait_recv()
    for j in range(nt):
        prepare_sources(j)

    mrun[...] = jnp.full(mrun.shape, -jnp.inf, f32)
    lrun[...] = jnp.zeros(lrun.shape, f32)
    chunk = min(512, rows)

    def row_pass(slot):
        for c in range(rows // chunk):
            at = slice(c * chunk, (c + 1) * chunk)
            old = mrun[:, at]
            top = old
            for r in range(blk // 8):
                rs = slice(8 * r, 8 * r + 8)
                top = jnp.maximum(top, sbuf[slot, rs, at] + wide(bcol[slot, rs, :], chunk // LANES))
            total = lrun[:, at] * jnp.exp2(old - top)
            for r in range(blk // 8):
                rs = slice(8 * r, 8 * r + 8)
                total = total + jnp.exp2(sbuf[slot, rs, at] + (wide(bcol[slot, rs, :], chunk // LANES) - top))
            mrun[:, at] = top
            lrun[:, at] = total

    scores(0, 0)

    def row_steps(pair, carry):
        for slot in range(2):
            k = 2 * pair + slot + 1
            wait_y(k)
            prepare_targets(k, 1 - slot)
            scores(k, 1 - slot)
            row_pass(slot)
        return carry

    lax.fori_loop(0, ns // 2 - 1, row_steps, 0)
    wait_y(ns - 1)
    prepare_targets(ns - 1, 1)
    scores(ns - 1, 1)
    row_pass(0)
    row_pass(1)

    top = jnp.max(mrun[...], axis=0, keepdims=True)
    rowstat[q, 0:1, :] = top
    rowstat[q, 1:2, :] = jnp.sum(lrun[...] * jnp.exp2(mrun[...] - top), axis=0, keepdims=True)
    for k in tsteps:
        r_copy(k, q, tgt_peer(k, 1)).start()
    scores(0, 0)
    for k in tsteps:
        r_copy(k, tgt_peer(k, -1), tgt_peer(k, 1)).wait_recv()
    top = rowstat[0, 0:1, :]
    for j in range(1, nt):
        top = jnp.maximum(top, rowstat[j, 0:1, :])
    total = jnp.zeros_like(top)
    for j in range(nt):
        total = total + rowstat[j, 1:2, :] * jnp.exp2(rowstat[j, 0:1, :] - top)
    lse = top + jnp.log(total) * LOG2E
    arow[...] = jnp.broadcast_to(LOG2E * la_ref[...] - lse, arow.shape)
    x = xall[...]
    f_ref[...] = epsilon * la_ref[...] - (epsilon * LN2) * lse + jnp.sum(x * x, axis=0, keepdims=True)

    def expos(k, slot):
        tops = sbuf[slot, :, 0:LANES] + arow[0:1, 0:LANES]
        for c in range(1, rows // LANES):
            at = slice(c * LANES, (c + 1) * LANES)
            tops = jnp.maximum(tops, sbuf[slot, :, at] + arow[0:1, at])
        mcol[...] = jnp.broadcast_to(jnp.max(tops, axis=1, keepdims=True), mcol.shape)
        for r in range(blk // 32):
            rs = slice(32 * r, 32 * r + 32)
            to = pl.ds(pl.multiple_of(k * blk + 32 * r, 32), 32)
            for c in range(rows // chunk):
                at = slice(c * chunk, (c + 1) * chunk)
                e = jnp.exp2(sbuf[slot, rs, at] + (arow[0:1, at] - wide(mcol[rs, :], chunk // LANES)))
                high = e.astype(bf16)
                ehi[to, at] = high
                elo[to, at] = ((e - high.astype(f32)) * LO_SCALE).astype(f8)

    def pull(k):
        at = pl.ds(pl.multiple_of(k * blk, blk), blk)
        main = jnp.dot(ehi[at, :], w[...], preferred_element_type=f32)
        rest = jnp.dot(elo[at, :], w8[...], preferred_element_type=f32)
        first = lax.broadcasted_iota(jnp.int32, (blk, LANES), 1) == 0
        sums = main[:, 0:LANES].T
        rest = rest.T
        stats = jnp.where(first, mcol[...], main[:, LANES : 2 * LANES]).T
        pulled[k] = sums[0:width] + sums[width : 2 * width] + rest[0:width] * (1.0 / (LO_SCALE * PT_SCALE))
        owner = lanes(src_peer(k, -1))
        colstat[p, 0:1, owner] = stats[0:1, :]
        colstat[p, 1:2, owner] = stats[1:2, :] + rest[width : width + 1, :] * (1.0 / LO_SCALE)

    def col_steps(pair, carry):
        for slot in range(2):
            k = 2 * pair + slot
            scores(k + 1, 1 - slot)
            expos(k, slot)
            pull(k)
        return carry

    lax.fori_loop(0, ns // 2 - 1, col_steps, 0)
    scores(ns - 1, 1)
    expos(ns - 2, 0)
    pull(ns - 2)
    expos(ns - 1, 1)
    pull(ns - 1)

    for k in ssteps:
        c_copy(k, p, src_peer(k, 1)).start()
    for k in ssteps:
        c_copy(k, src_peer(k, -1), src_peer(k, 1)).wait_recv()
    top = colstat[0, 0:1, :]
    for j in range(1, ns):
        top = jnp.maximum(top, colstat[j, 0:1, :])
    total = jnp.zeros_like(top)
    for j in range(ns):
        total = total + colstat[j, 1:2, :] * jnp.exp2(colstat[j, 0:1, :] - top)
    lse = top + jnp.log(total) * LOG2E
    srow[0:1, :] = jnp.exp2(LOG2E * lb_ref[...] + (colstat[p, 0:1, :] - lse))
    go_ref[...] = epsilon * lb_ref[...] - (epsilon * LN2) * lse

    def weigh(k, carry):
        owner = lanes(src_peer(k, -1))
        at = pl.ds(pl.multiple_of(k * blk, blk), blk)
        s = srow[0:1, owner]
        y = yslots[k]
        go_ref[:, owner] = go_ref[:, owner] + jnp.sum(y * y, axis=0, keepdims=True)
        pulled[k] = pulled[k] * s
        ys = y * s
        high, low = split(ys)
        shigh, slow = split(jnp.broadcast_to(s, (8, blk)))
        left[:, at] = jnp.concatenate([high, low, shigh, slow], axis=0).astype(bf16)
        left8[:, at] = to_f8(jnp.concatenate([ys, jnp.broadcast_to(s, (32, blk))], axis=0) * PT_SCALE)
        if comm:

            @pl.when(k > 0)
            def _():
                gt_copy(k).start()

        return carry

    lax.fori_loop(0, ns, weigh, 0)

    def push(k):
        at = lanes(tgt_peer(k, -1))
        main = jnp.dot(left[...], ehi[:, at], preferred_element_type=f32)
        rest = jnp.dot(left8[...], elo[:, at], preferred_element_type=f32) * (1.0 / (LO_SCALE * PT_SCALE))
        moved = main[0:width] + main[width : 2 * width] + rest[0:width]
        mass = main[2 * width : 2 * width + 1] + main[2 * width + 8 : 2 * width + 9] + rest[width : width + 1]
        return 2.0 * (xall[:, at] * mass - moved)

    def push_step(k, carry):
        gsend[k] = push(k)
        if comm:
            gs_copy(k).start()
        return carry

    lax.fori_loop(1, nt, push_step, 0)
    grad = push(0)

    mine = lanes(p)
    moved = pulled[0]
    for k in range(1, ns):
        if comm:
            gt_copy(k).wait_recv()
        moved = moved + gtrecv[k]
    gt_ref[...] = 2.0 * (tgt_ref[...] * jnp.exp2(LOG2E * lb_ref[:, mine]) - moved)
    for k in range(1, nt):
        if comm:
            gs_copy(k).wait_recv()
        grad = grad + gsrecv[k]
    gs_ref[...] = grad

    for k in tsteps:
        x_copy(k, q, tgt_peer(k, 1)).wait_send()
        r_copy(k, q, tgt_peer(k, 1)).wait_send()
        gs_copy(k).wait_send()
    for k in ssteps:
        y_copy(k).wait_send()
        c_copy(k, p, src_peer(k, 1)).wait_send()
        gt_copy(k).wait_send()


def call(ns, ny, nt, nc, comm, width, blk):
    rows, cols = nt * blk, ns * blk
    vmem = pl.BlockSpec(memory_space=pltpu.VMEM)
    dma = pltpu.SemaphoreType.DMA
    scratch = [
        ((width, rows), f32), ((ns, width, blk), f32), ((4 * width, rows), bf16), ((cols, 2 * LANES), bf16),
        ((rows, 2 * LANES), bf16), ((rows, LANES), f8), ((2, blk, LANES), f32), ((2, blk, rows), f32),
        ((8, rows), f32), ((8, rows), f32), ((8, rows), f32), ((blk, LANES), f32),
        ((nt, 2, rows), f32), ((ns, 2, cols), f32), ((8, cols), f32),
        ((cols, rows), bf16), ((cols, rows), f8), ((ns, width, blk), f32),
        ((2 * width + 16, cols), bf16), ((width + 32, cols), f8),
        ((nt, width, blk), f32), ((nt, width, blk), f32), ((ns, width, blk), f32),
    ]
    sems = [nt, nt, ns, ns, nt, nt, ns, ns, nt, nt, ns, ns]
    params = dict(vmem_limit_bytes=60 * 2**20, has_side_effects=True)
    if comm:
        params["collective_id"] = 0
    return pl.pallas_call(
        functools.partial(kernel, ns, ny, nt, nc, comm),
        out_shape=[
            jax.ShapeDtypeStruct((1, rows), f32),
            jax.ShapeDtypeStruct((1, cols), f32),
            jax.ShapeDtypeStruct((width, blk), f32),
            jax.ShapeDtypeStruct((width, blk), f32),
        ],
        in_specs=[vmem] * 5,
        out_specs=[vmem] * 4,
        scratch_shapes=[pltpu.VMEM(*s) for s in scratch] + [dma((n,)) for n in sems],
        compiler_params=pltpu.CompilerParams(**params),
        name="sinkhorn",
    )


def solution(mesh):
    ns, nt = mesh.shape["src"], mesh.shape["tgt"]
    ny = 4 if ns % 4 == 0 else 1
    nc = 2 if nt % 2 == 0 else 1

    def per_device(src_points, tgt_points, log_a, log_b, g_init):
        width, blk = src_points.shape
        run = call(ns, ny, nt, nc, True, width, blk)
        f, g, grad_src, grad_tgt = run(
            src_points, tgt_points, log_a.reshape(1, -1), log_b.reshape(1, -1), g_init.reshape(1, -1)
        )
        return f.reshape(-1), g.reshape(-1), grad_src, grad_tgt

    in_specs = (P(None, ("src", "tgt")), P(None, ("tgt", "src")), P("src"), P("tgt"), P("tgt"))
    out_specs = (P("src"), P("tgt"), P(None, ("src", "tgt")), P(None, ("tgt", "src")))
    return jax.shard_map(per_device, mesh=mesh, in_specs=in_specs, out_specs=out_specs, check_vma=False)
```

time: 530 us -> 88.4 us (0.17); the launches traced: 520 us -> 87.2 us
  matrix products: 173 us -> 0 us
  waiting for transfers between devices: 158 us -> 0 us
  blocking collectives: 156 us -> 0 us
  Pallas kernels: 0 us -> 82.5 us
  other arithmetic: 14.3 us -> 0 us
  between operations: 14.3 us -> 0.65 us
    dot_general x20 -> x0, matrix products: 173 us -> none  [the longest x12 118 us: tile_at(): lax.dot_general(src_part, targets, (((0,), (0,)), ((), ())), precision=hi...]
    reduce_scatter x2 -> x0, waiting for transfers between devices: 124 us -> none  [the longest x1 77.2 us: per_device(): lax.psum_scatter(2.0 * (targets * col_mass[None, :] - pulled), 'src', sca...]
    pallas_call x0 -> x1, Pallas kernels: none -> 82.5 us  [per_device(): run(src_points, tgt_points, log_a.reshape(1, -1), log_b.reshape(1, -1), g...]
    pmax x2 -> x0, blocking collectives: 71.9 us -> none  [the longest x1 57.9 us: per_device(): col_peak = lax.pmax(local_peak, 'src')]
    psum x2 -> x0, blocking collectives: 69.5 us -> none  [the longest x1 55.9 us: per_device(): col_total = lax.psum(local_total * jnp.exp(local_peak - col_peak), 'src')]
    all_gather x1 -> x0, waiting for transfers between devices: 32.4 us -> none  [per_device(): targets = lax.all_gather(tgt_points, 'src', axis=1, tiled=True)]
    all_gather x1 -> x0, blocking collectives: 15 us -> none  [per_device(): sources = lax.all_gather(src_points, 'tgt', axis=1, tiled=True)]
    reduce_sum x10 -> x0, other arithmetic: 11.8 us -> none  [the longest x4 5.3 us: column_step(): total = total * factor + jnp.sum(expos, axis=0)]
  transfers between devices with their start and end apart: 3 -> 0, of which waited for: 3 -> 0; matrix products, arithmetic and copies ran while one was open for 0% -> 0% of each run, Pallas kernels for 0% -> 0%
where the time goes in v1:
time: 88.4 us; the launch traced here: 87.2 us
  Pallas kernels  82.5 us (93%)
  local copies, waits for them, and re-layouts  4.05 us (5%)
    pallas_call x1, Pallas kernels, per_device(): run(src_points, tgt_points, log_a.reshape(1, -1), log_b.reshape(1, -1), g...  82.5 us
    unnamed x8, local copies, waits for them, and re-layouts  4.05 us

profile of v1, /device:TPU:1, one launch (start us, length us, event | category | flops | bytes accessed | tf_op | source)
XLA Modules:
  0.0 87.2 jit_solution(10956783471072779941)
XLA Ops:
  0.6 82.5 %sinkhorn.1 = (f32[1,2048]{1,0:T(1,128)}, f32[1,4096]{1,0:T(1,128)}, f32[64,256]{1,0:T(8,128)}, f32[64,256]{1,0:T(8,128)}) custom-call(f32[64,256]{1,0:T(8,128)} %src_ref.1, f32[64,256]{1,0:T(8,128)} %tgt_ref.1, f32[1,2048]{1,0:T(1,128)} %bitcast.9, f32[1,4096]{1,0:T(1,128)} %bitcast.6, f32[1,4096]{1,0:T(1,128)} %bitcast.7), custom_call_target="tpu_custom_call" | custom-call | tf_op jit(solution)/shard_map/sinkhorn/pallas_call | solution.py:361
  83.1 0.0 copy-start.1
  83.1 1.3 %copy.13 = f32[2048]{0:T(1024)} copy(f32[2048]{0:T(1024)} %bitcast.8) | data formatting | bytes 16384
  84.4 0.0 copy-done.1
  84.4 0.6 copy.14
  85.0 0.0 copy-start
  85.0 1.5 %copy.15 = f32[64,256]{1,0:T(8,128)} copy(f32[64,256]{1,0:T(8,128)} %get-tuple-element.18) | data formatting | bytes 131072
  86.5 0.0 copy-done
  86.5 0.6 copy.16
Async XLA Ops:
  83.1 1.3 %copy-start.1 = (f32[1,4096]{1,0:T(1,128)S(1)}, f32[1,4096]{1,0:T(1,128)}, u32[]{:S(2)}) copy-start(f32[1,4096]{1,0:T(1,128)} %get-tuple-element.9) | copy-start | bytes 49156
  85.0 1.5 %copy-start = (f32[64,256]{1,0:T(8,128)S(1)}, f32[64,256]{1,0:T(8,128)}, u32[]{:S(2)}) copy-start(f32[64,256]{1,0:T(8,128)} %get-tuple-element.19) | copy-start | bytes 196612

commit v2 on v1

v2 whole, which is shorter than its diff:
```python
import functools

import jax
import jax.numpy as jnp
from jax import lax
from jax.experimental import pallas as pl
from jax.experimental.pallas import tpu as pltpu
from jax.sharding import PartitionSpec as P

epsilon = 0.5
LOG2E = 1.4426950408889634
LN2 = 0.6931471805599453
SCALE = LOG2E / epsilon
LIFT = 17.0
PT_SCALE = 2.0**4
F8_MAX = 448.0
MESH = pl.DeviceIdType.MESH
f32, bf16, f8 = jnp.float32, jnp.bfloat16, jnp.float8_e4m3fn
LANES = 128


def split(value):
    high = value.astype(bf16).astype(f32)
    return high, value - high


def to_f8(value):
    return jnp.clip(value, -F8_MAX, F8_MAX).astype(f8)


def wide(column, times):
    return jnp.concatenate([column] * times, axis=1)


def column_parts(ns):
    cuts = [0, 6, 12, 16] if ns == 16 else [0, ns // 2, ns]
    return list(zip(cuts[:-1], cuts[1:]))


def kernel(
    ns, ny, nt, nc, comm,
    src_ref, tgt_ref, la_ref, lb_ref, g_ref,
    f_ref, go_ref, gs_ref, gt_ref,
    xall, yslots, xs, yt, w, w8, bcol, sbuf, mrun, lrun, arow, mcol, rowstat, colstat, srow,
    ehi, elo, pulled, left, left8, gsend, gsrecv, gtrecv,
    sx, rx, sy, ry, sr, rr, sc, rc, sgs, rgs, sgt, rgt,
):
    blk = src_ref.shape[1]
    width = src_ref.shape[0]
    rows, cols = nt * blk, ns * blk
    parts = column_parts(ns)
    if comm:
        p, q = lax.axis_index("src"), lax.axis_index("tgt")
    else:
        p, q = jnp.int32(0), jnp.int32(0)

    def shifted(at, step, count, minor, sign):
        major = count // minor
        a = lax.rem(at // minor + sign * (step // minor) + major, major)
        b = lax.rem(lax.rem(at, minor) + sign * lax.rem(step, minor) + minor, minor)
        return a * minor + b

    def src_peer(step, sign):
        return shifted(p, jnp.int32(step), ns, ny, sign)

    def tgt_peer(step, sign):
        return shifted(q, jnp.int32(step), nt, nc, sign)

    def lanes(owner):
        return pl.ds(pl.multiple_of(owner * blk, blk), blk)

    def remote(source, target, send, recv, device):
        return pltpu.make_async_remote_copy(
            src_ref=source, dst_ref=target, send_sem=send, recv_sem=recv, device_id=device, device_id_type=MESH
        )

    tsteps = range(1, nt) if comm else ()
    ssteps = range(1, ns) if comm else ()
    near = [d for d in (1, ny - 1, 2) if d < ny]
    near_z = [d for d in near if d < ns // ny]


    nz, nx = ns // ny, nt // nc

    def x_copy(k):
        dx, dc = k // nc, k % nc
        if dc == 0 or dx == 0:
            return remote(src_ref, xall.at[:, lanes(q)], sx.at[k], rx.at[k], (p, tgt_peer(k, 1)))
        at = lanes(tgt_peer(dx * nc, -1))
        return remote(xall.at[:, at], xall.at[:, at], sx.at[k], rx.at[k], (p, tgt_peer(dc, 1)))

    def y_copy(k, h):
        dz, dy = k // ny, k % ny
        at, sem = pl.ds(h * (width // 2), width // 2), h * ns + k
        if dz == 0 or dy == 0:
            source, to = tgt_ref.at[at, :], src_peer(k, 1)
        elif h == 0:
            source, to = yslots.at[dz * ny, at, :], src_peer(dy, 1)
        else:
            source, to = yslots.at[dy, at, :], src_peer(dz * ny, 1)
        return remote(source, yslots.at[k, at, :], sy.at[sem], ry.at[sem], (to, q))

    def r_copy(k, owner, to):
        return remote(rowstat.at[q], rowstat.at[owner], sr.at[k], rr.at[k], (p, to))

    def c_copy(part, k, owner, to):
        at = slice(parts[part][0] * blk, parts[part][1] * blk)
        sem = part * ns + k
        return remote(colstat.at[p, :, at], colstat.at[owner, :, at], sc.at[sem], rc.at[sem], (to, q))

    major = ns // ny
    back_z = [lax.rem(t - p // ny + major, major) for t in range(major)]
    back_y = [lax.rem(t - lax.rem(p, ny) + ny, ny) for t in range(ny)]
    block_z = [lax.rem(p // ny - t + major, major) for t in range(major)]
    block_y = [lax.rem(lax.rem(p, ny) - t + ny, ny) for t in range(ny)]

    def place(j, k):
        return back_z[(j // ny + k // ny) % major] * ny + back_y[(j % ny + k % ny) % ny]

    def gs_copy(k):
        return remote(gsend.at[k], gsrecv.at[k], sgs.at[k], rgs.at[k], (p, tgt_peer(k, -1)))

    def gt_copy(k):
        return remote(pulled.at[k], gtrecv.at[k], sgt.at[k], rgt.at[k], (src_peer(k, -1), q))

    if comm:
        barrier = pltpu.get_barrier_semaphore()
        for k in tsteps:
            pl.semaphore_signal(barrier, inc=1, device_id=(p, tgt_peer(k, 1)), device_id_type=MESH)
        for k in ssteps:
            pl.semaphore_signal(barrier, inc=1, device_id=(src_peer(k, 1), q), device_id_type=MESH)
        pl.semaphore_wait(barrier, nt - 1 + ns - 1)

    if comm:
        for k in [dx * nc for dx in (1, 3, 2) if dx < nx] + list(range(1, nc)):
            x_copy(k).start()
        for dz in near_z:
            y_copy(dz * ny, 0).start()
        for dy in near:
            y_copy(dy, 1).start()
        for dz in near_z:
            y_copy(dz * ny, 1).start()
        for dy in near:
            y_copy(dy, 0).start()
    xall[:, lanes(q)] = src_ref[...]
    yslots[0] = tgt_ref[...]

    def prepare_targets(k, slot):
        y = yslots[k]
        scaled = y * (2.0 * SCALE)
        parts = jnp.concatenate(split(scaled), axis=0).T.astype(bf16)
        at = pl.ds(pl.multiple_of(k * blk, blk), blk)
        yt[at, 0:LANES] = parts
        yt[at, LANES : 2 * LANES] = parts
        bias = SCALE * (g_ref[:, lanes(src_peer(k, -1))] - jnp.sum(y * y, axis=0, keepdims=True))
        bcol[slot] = jnp.broadcast_to(bias, (LANES, blk)).T

    def prepare_sources(j):
        at = pl.ds(j * blk, blk)
        x = xall[:, at]
        high, low = split(x)
        xs[0:width, at] = high.astype(bf16)
        xs[width : 2 * width, at] = high.astype(bf16)
        xs[2 * width : 3 * width, at] = low.astype(bf16)
        xs[3 * width : 4 * width, at] = low.astype(bf16)
        w[at, 0:LANES] = jnp.concatenate([high, low], axis=0).T.astype(bf16)
        w[at, LANES : 2 * LANES] = jnp.ones((blk, LANES), bf16)
        parts = jnp.concatenate([x * PT_SCALE, jnp.ones_like(x)], axis=0).T
        w8[at, :] = to_f8(parts)

    chunk = min(512, rows)

    def scores(k, slot, c):
        at = slice(k * blk, (k + 1) * blk) if isinstance(k, int) else lanes(k)
        to = slice(c * chunk, (c + 1) * chunk)
        sbuf[slot, :, to] = jnp.dot(yt[at, :], xs[:, to], preferred_element_type=f32)

    def wait_y(k):
        if comm and near_z:

            @pl.when(jnp.logical_and(k // ny > 0, lax.rem(k, ny) > 0))
            def _():
                for h in range(2):
                    at, sem = pl.ds(h * (width // 2), width // 2), h * ns + k
                    remote(
                        tgt_ref.at[at, :], yslots.at[k, at, :], sy.at[sem], ry.at[sem], (src_peer(k, 1), q)
                    ).wait_recv()

    prepare_targets(0, 0)
    if comm:
        for k in [dx * nc for dx in (1, 3, 2) if dx < nx]:
            x_copy(k).wait_recv()
            for dc in range(1, nc):
                x_copy(k + dc).start()
        for dz, dy in zip(near_z + [0] * (len(near) - len(near_z)), near):
            if dz:
                y_copy(dz * ny, 0).wait_recv()
                for to in near:
                    y_copy(dz * ny + to, 0).start()
            y_copy(dy, 1).wait_recv()
            for to in near_z:
                y_copy(to * ny + dy, 1).start()
        for dz in near_z:
            y_copy(dz * ny, 1).wait_recv()
        for dy in near:
            y_copy(dy, 0).wait_recv()
        for dc in range(1, nc):
            for dx in [0] + [d for d in (1, 3, 2) if d < nx]:
                x_copy(dx * nc + dc).wait_recv()
    for j in range(nt):
        prepare_sources(j)

    mrun[...] = jnp.full(mrun.shape, -jnp.inf, f32)
    lrun[...] = jnp.zeros(lrun.shape, f32)
    def row_pass(slot, c):
        if True:
            at = slice(c * chunk, (c + 1) * chunk)
            old = mrun[:, at]
            top = old
            for r in range(blk // 8):
                rs = slice(8 * r, 8 * r + 8)
                top = jnp.maximum(top, sbuf[slot, rs, at] + wide(bcol[slot, rs, :], chunk // LANES))
            total = lrun[:, at] * jnp.exp2(old - top)
            for r in range(blk // 8):
                rs = slice(8 * r, 8 * r + 8)
                total = total + jnp.exp2(sbuf[slot, rs, at] + (wide(bcol[slot, rs, :], chunk // LANES) - top))
            mrun[:, at] = top
            lrun[:, at] = total

    steps = range(rows // chunk)

    def row_step(k, slot):
        wait_y(k + 1)
        prepare_targets(k + 1, 1 - slot)
        for c in steps:
            scores(k + 1, 1 - slot, c)
            row_pass(slot, c)

    def row_steps(pair, carry):
        row_step(2 * pair, 0)
        row_step(2 * pair + 1, 1)
        return carry

    for c in steps:
        scores(0, 0, c)
    lax.fori_loop(0, ns // 2 - 1, row_steps, 0)
    row_step(jnp.int32(ns - 2), 0)
    for c in steps:
        row_pass(1, c)

    top = jnp.max(mrun[...], axis=0, keepdims=True)
    rowstat[q, 0:1, :] = top
    rowstat[q, 1:2, :] = jnp.sum(lrun[...] * jnp.exp2(mrun[...] - top), axis=0, keepdims=True)
    for k in tsteps:
        r_copy(k, q, tgt_peer(k, 1)).start()
    for c in steps:
        scores(0, 0, c)
    for k in tsteps:
        r_copy(k, tgt_peer(k, -1), tgt_peer(k, 1)).wait_recv()
    top = rowstat[0, 0:1, :]
    for j in range(1, nt):
        top = jnp.maximum(top, rowstat[j, 0:1, :])
    total = jnp.zeros_like(top)
    for j in range(nt):
        total = total + rowstat[j, 1:2, :] * jnp.exp2(rowstat[j, 0:1, :] - top)
    lse = top + jnp.log(total) * LOG2E
    arow[...] = jnp.broadcast_to(LOG2E * la_ref[...] - lse, arow.shape)
    x = xall[...]
    f_ref[...] = epsilon * la_ref[...] - (epsilon * LN2) * lse + jnp.sum(x * x, axis=0, keepdims=True)

    quarter = blk // 4

    def tops(slot, piece):
        rs = slice(piece * quarter, (piece + 1) * quarter)
        top = sbuf[slot, rs, 0:LANES] + arow[0:1, 0:LANES]
        for c in range(1, rows // LANES):
            at = slice(c * LANES, (c + 1) * LANES)
            top = jnp.maximum(top, sbuf[slot, rs, at] + arow[0:1, at])
        top = jnp.max(top, axis=1, keepdims=True) - LIFT
        mcol[slot, rs, :] = jnp.broadcast_to(top, (quarter, LANES))

    def expos(k, slot, piece):
        for r in range(piece * quarter, (piece + 1) * quarter, 32):
            rs = slice(r, r + 32)
            to = slice(k * blk + r, k * blk + r + 32)
            for c in steps:
                at = slice(c * chunk, (c + 1) * chunk)
                e = jnp.exp2(sbuf[slot, rs, at] + (arow[0:1, at] - wide(mcol[slot, rs, :], chunk // LANES)))
                high = e.astype(bf16)
                low = (e - high.astype(f32)).astype(f8)
                ehi[to, at] = high
                elo[to, at] = low

    half = rows // 2

    def pull_product(k, piece):
        rs = slice(k * blk, (k + 1) * blk)
        at = slice(piece % 2 * half, (piece % 2 + 1) * half)
        if piece < 2:
            return jnp.dot(ehi[rs, at], w[at, :], preferred_element_type=f32)
        return jnp.dot(elo[rs, at], w8[at, :], preferred_element_type=f32)

    def pull_finish(k, products):
        main = products[0] + products[1]
        rest = (products[2] + products[3]).T
        first = lax.broadcasted_iota(jnp.int32, (blk, LANES), 1) == 0
        sums = main[:, 0:LANES].T
        stats = jnp.where(first, mcol[2], main[:, LANES : 2 * LANES]).T
        pulled[k] = sums[0:width] + sums[width : 2 * width] + rest[0:width] * (1.0 / PT_SCALE)
        at = slice(k * blk, (k + 1) * blk)
        colstat[p, 0:1, at] = stats[0:1, :]
        colstat[p, 1:2, at] = stats[1:2, :] + rest[width : width + 1, :]

    def turn(k, slot, pulls=True, exps=True, finds=True):
        products = []
        if pulls:
            mcol[2] = mcol[1 - slot]
        for piece in range(4):
            if finds and piece < len(steps):
                scores(k + 1, 1 - slot, piece)
            if pulls:
                products.append(pull_product(k - 1, piece))
            if exps:
                expos(k, slot, piece)
        if pulls:
            pull_finish(k - 1, products)
        if finds:
            for piece in range(4):
                tops(1 - slot, piece)

    def send_stats(part):
        for k in ssteps:
            c_copy(part, k, p, src_peer(k, 1)).start()

    def send_pulled(k, carry):
        gt_copy(k).start()
        return carry

    for piece in range(4):
        tops(0, piece)
    sent, part = 1, 0
    for k in range(ns + 1):
        turn(k, k % 2, pulls=k > 0, exps=k < ns, finds=k + 1 < ns)
        if k == parts[part][1]:
            send_stats(part)
            part += 1
            if comm:
                lax.fori_loop(sent, k, send_pulled, 0)
                sent = k

    for part in range(len(parts)):
        for k in ssteps:
            c_copy(part, k, src_peer(k, -1), src_peer(k, 1)).wait_recv()

    def weigh(k):
        owner = lanes(block_z[k // ny] * ny + block_y[k % ny])
        spots = [lanes(place(j, k)) for j in range(ns)]
        tops = [colstat[j, 0:1, spots[j]] for j in range(ns)]
        top = functools.reduce(jnp.maximum, tops)
        total = jnp.zeros_like(top)
        for j in range(ns):
            total = total + colstat[j, 1:2, spots[j]] * jnp.exp2(tops[j] - top)
        lse = top + jnp.log(total) * LOG2E
        y = yslots[k]
        weight = LOG2E * lb_ref[:, owner] - lse
        srow[0:1, owner] = weight
        square = jnp.sum(y * y, axis=0, keepdims=True)
        go_ref[:, owner] = epsilon * lb_ref[:, owner] - (epsilon * LN2) * lse + square
        at = slice(k * blk, (k + 1) * blk)
        s = jnp.exp2(weight + colstat[p, 0:1, at])
        ys = y * s
        high, low = split(ys)
        shigh, slow = split(jnp.broadcast_to(s, (8, blk)))
        left[:, at] = jnp.concatenate([high, low, shigh, slow], axis=0).astype(bf16)
        left8[:, at] = to_f8(jnp.concatenate([ys, jnp.broadcast_to(s, (32, blk))], axis=0) * (PT_SCALE * 2.0**LIFT))

    for k in range(ns):
        weigh(k)

    def push(k):
        at = lanes(tgt_peer(k, -1))
        main = jnp.dot(left[...], ehi[:, at], preferred_element_type=f32)
        rest = jnp.dot(left8[...], elo[:, at], preferred_element_type=f32) * (1.0 / (PT_SCALE * 2.0**LIFT))
        moved = main[0:width] + main[width : 2 * width] + rest[0:width]
        mass = main[2 * width : 2 * width + 1] + main[2 * width + 8 : 2 * width + 9] + rest[width : width + 1]
        return 2.0 * (xall[:, at] * mass - moved)

    def push_step(k, carry):
        gsend[k] = push(k)
        if comm:
            gs_copy(k).start()
        return carry

    lax.fori_loop(1, nt, push_step, 0)
    grad = push(0)

    mine = lanes(p)
    weight = srow[0:1, mine]
    moved = pulled[0] * jnp.exp2(weight + colstat[p, 0:1, 0:blk])
    for k in range(1, ns):
        if comm:
            gt_copy(k).wait_recv()
        moved = moved + gtrecv[k] * jnp.exp2(weight + colstat[src_peer(k, 1), 0:1, k * blk : (k + 1) * blk])
    gt_ref[...] = 2.0 * (tgt_ref[...] * jnp.exp2(LOG2E * lb_ref[:, mine]) - moved)
    for k in range(1, nt):
        if comm:
            gs_copy(k).wait_recv()
        grad = grad + gsrecv[k]
    gs_ref[...] = grad

    for k in tsteps:
        x_copy(k).wait_send()
        r_copy(k, q, tgt_peer(k, 1)).wait_send()
        gs_copy(k).wait_send()
    for k in ssteps:
        for h in range(2):
            y_copy(k, h).wait_send()
        for part in range(len(parts)):
            c_copy(part, k, p, src_peer(k, 1)).wait_send()
        gt_copy(k).wait_send()


def hand_out(*refs):
    for source, target in zip(refs[:4], refs[4:]):
        target[...] = source[...]


def call(ns, ny, nt, nc, comm, width, blk):
    rows, cols = nt * blk, ns * blk
    vmem = pl.BlockSpec(memory_space=pltpu.VMEM)
    dma = pltpu.SemaphoreType.DMA
    scratch = [
        ((width, rows), f32), ((ns, width, blk), f32), ((4 * width, rows), bf16), ((cols, 2 * LANES), bf16),
        ((rows, 2 * LANES), bf16), ((rows, LANES), f8), ((2, blk, LANES), f32), ((2, blk, rows), f32),
        ((8, rows), f32), ((8, rows), f32), ((8, rows), f32), ((3, blk, LANES), f32),
        ((nt, 2, rows), f32), ((ns, 2, cols), f32), ((8, cols), f32),
        ((cols, rows), bf16), ((cols, rows), f8), ((ns, width, blk), f32),
        ((2 * width + 16, cols), bf16), ((width + 32, cols), f8),
        ((nt, width, blk), f32), ((nt, width, blk), f32), ((ns, width, blk), f32),
    ]
    waits = len(column_parts(ns)) * ns
    sems = [nt, nt, 2 * ns, 2 * ns, nt, nt, waits, waits, nt, nt, ns, ns]
    params = dict(vmem_limit_bytes=60 * 2**20, has_side_effects=True)
    if comm:
        params["collective_id"] = 0
    return pl.pallas_call(
        functools.partial(kernel, ns, ny, nt, nc, comm),
        out_shape=[
            jax.ShapeDtypeStruct((1, rows), f32),
            jax.ShapeDtypeStruct((1, cols), f32),
            jax.ShapeDtypeStruct((width, blk), f32),
            jax.ShapeDtypeStruct((width, blk), f32),
        ],
        in_specs=[vmem] * 5,
        out_specs=[vmem] * 4,
        scratch_shapes=[pltpu.VMEM(*s) for s in scratch] + [dma((n,)) for n in sems],
        compiler_params=pltpu.CompilerParams(**params),
        name="sinkhorn",
    )


def solution(mesh):
    ns, nt = mesh.shape["src"], mesh.shape["tgt"]
    ny = 4 if ns % 4 == 0 else 1
    nc = 2 if nt % 2 == 0 else 1

    def per_device(src_points, tgt_points, log_a, log_b, g_init):
        width, blk = src_points.shape
        run = call(ns, ny, nt, nc, True, width, blk)
        f, g, grad_src, grad_tgt = run(
            src_points, tgt_points, log_a.reshape(1, -1), log_b.reshape(1, -1), g_init.reshape(1, -1)
        )
        vmem = pl.BlockSpec(memory_space=pltpu.VMEM)
        outs = (f, g, grad_src, grad_tgt)
        f, g, grad_src, grad_tgt = pl.pallas_call(
            hand_out,
            out_shape=[jax.ShapeDtypeStruct(o.shape, o.dtype) for o in outs],
            in_specs=[vmem] * 4,
            out_specs=[vmem] * 4,
            name="results",
        )(*outs)
        return f.reshape(-1), g.reshape(-1), grad_src, grad_tgt

    in_specs = (P(None, ("src", "tgt")), P(None, ("tgt", "src")), P("src"), P("tgt"), P("tgt"))
    out_specs = (P("src"), P("tgt"), P(None, ("src", "tgt")), P(None, ("tgt", "src")))
    return jax.shard_map(per_device, mesh=mesh, in_specs=in_specs, out_specs=out_specs, check_vma=False)
```

time: 88.4 us -> 79.6 us (0.900); the launches traced: 87.2 us -> 79.4 us
  local copies, waits for them, and re-layouts: 4.05 us -> 0 us
  Pallas kernels: 82.5 us -> 78.8 us
    pallas_call x1, Pallas kernels: 82.5 us -> 77.2 us  [per_device(): run(src_points, tgt_points, log_a.reshape(1, -1), log_b.reshape(1, -1), g...]
    unnamed x8 -> x0, local copies, waits for them, and re-layouts: 4.05 us -> none
    pallas_call x0 -> x1, Pallas kernels: none -> 1.57 us  [per_device(): pl.pallas_call(hand_out, out_shape=[jax.ShapeDtypeStruct(o.shape, o.dtype...]
where the time goes in v2:
time: 79.6 us; the launch traced here: 79.4 us
  Pallas kernels  78.8 us (99%)
    pallas_call x1, Pallas kernels, per_device(): run(src_points, tgt_points, log_a.reshape(1, -1), log_b.reshape(1, -1), g...  77.2 us

profile of v2, /device:TPU:1, one launch (start us, length us, event | category | flops | bytes accessed | tf_op | source)
XLA Modules:
  0.0 79.4 jit_solution(11224299610960166512)
XLA Ops:
  0.6 77.2 %sinkhorn.1 = (f32[1,2048]{1,0:T(1,128)}, f32[1,4096]{1,0:T(1,128)}, f32[64,256]{1,0:T(8,128)}, f32[64,256]{1,0:T(8,128)}) custom-call(f32[64,256]{1,0:T(8,128)} %src_ref.1, f32[64,256]{1,0:T(8,128)} %tgt_ref.1, f32[1,2048]{1,0:T(1,128)} %bitcast.7, f32[1,4096]{1,0:T(1,128)} %bitcast.5, f32[1,4096]{1,0:T(1,128)} %bitcast.6), custom_call_target="tpu_custom_call" | custom-call | tf_op jit(solution)/shard_map/sinkhorn/pallas_call | solution.py:470
  77.8 1.6 %results.1 = (f32[1,2048]{1,0:T(1,128)}, f32[1,4096]{1,0:T(1,128)}, f32[64,256]{1,0:T(8,128)}, f32[64,256]{1,0:T(8,128)}) custom-call(f32[1,2048]{1,0:T(1,128)} %get-tuple-element.12.refs_0_, f32[1,4096]{1,0:T(1,128)} %get-tuple-element.13.refs_1_, f32[64,256]{1,0:T(8,128)} %get-tuple-element.14.refs_2_, f32[64,256]{1,0:T(8,128)} %get-tuple-element.15.refs_3_), custom_call_target="tpu_custom_call" | custom-call | tf_op jit(solution)/shard_map/results/pallas_call | solution.py:475

commit v3 on v2

--- a/solution.py
+++ b/solution.py
@@ -41,7 +41,7 @@
     ns, ny, nt, nc, comm,
     src_ref, tgt_ref, la_ref, lb_ref, g_ref,
     f_ref, go_ref, gs_ref, gt_ref,
-    xall, yslots, xs, yt, w, w8, bcol, sbuf, mrun, lrun, arow, mcol, rowstat, colstat, srow,
+    xall, yslots, xs, yt, w, w8, bcol, sbuf, table, mrun, lrun, arow, mcol, rowstat, colstat, srow,
     ehi, elo, pulled, left, left8, gsend, gsrecv, gtrecv,
     sx, rx, sy, ry, sr, rr, sc, rc, sgs, rgs, sgt, rgt,
 ):
@@ -170,10 +170,18 @@
 
     chunk = min(512, rows)
 
-    def scores(k, slot, c):
+    kept = 1 + 2 * (ns // 8)
+
+    def scores(k, slot, c, keep=False):
         at = slice(k * blk, (k + 1) * blk) if isinstance(k, int) else lanes(k)
         to = slice(c * chunk, (c + 1) * chunk)
-        sbuf[slot, :, to] = jnp.dot(yt[at, :], xs[:, to], preferred_element_type=f32)
+        value = jnp.dot(yt[at, :], xs[:, to], preferred_element_type=f32)
+        sbuf[slot, :, to] = value
+        if keep:
+            table[k, :, to] = value
+
+    def held(k, slot):
+        return table.at[k] if k < kept else sbuf.at[slot]
 
     def wait_y(k):
         if comm and near_z:
@@ -229,22 +237,23 @@
 
     steps = range(rows // chunk)
 
-    def row_step(k, slot):
+    def row_step(k, slot, keep):
         wait_y(k + 1)
         prepare_targets(k + 1, 1 - slot)
         for c in steps:
-            scores(k + 1, 1 - slot, c)
+            scores(k + 1, 1 - slot, c, keep)
             row_pass(slot, c)
 
-    def row_steps(pair, carry):
-        row_step(2 * pair, 0)
-        row_step(2 * pair + 1, 1)
+    def row_steps(keep, pair, carry):
+        row_step(2 * pair, 0, keep)
+        row_step(2 * pair + 1, 1, keep)
         return carry
 
     for c in steps:
-        scores(0, 0, c)
-    lax.fori_loop(0, ns // 2 - 1, row_steps, 0)
-    row_step(jnp.int32(ns - 2), 0)
+        scores(0, 0, c, True)
+    lax.fori_loop(0, kept // 2, functools.partial(row_steps, True), 0)
+    lax.fori_loop(kept // 2, ns // 2 - 1, functools.partial(row_steps, False), 0)
+    row_step(jnp.int32(ns - 2), 0, False)
     for c in steps:
         row_pass(1, c)
 
@@ -253,8 +262,6 @@
     rowstat[q, 1:2, :] = jnp.sum(lrun[...] * jnp.exp2(mrun[...] - top), axis=0, keepdims=True)
     for k in tsteps:
         r_copy(k, q, tgt_peer(k, 1)).start()
-    for c in steps:
-        scores(0, 0, c)
     for k in tsteps:
         r_copy(k, tgt_peer(k, -1), tgt_peer(k, 1)).wait_recv()
     top = rowstat[0, 0:1, :]
@@ -270,22 +277,24 @@
 
     quarter = blk // 4
 
-    def tops(slot, piece):
+    def tops(k, slot, piece):
+        source = held(k, slot)
         rs = slice(piece * quarter, (piece + 1) * quarter)
-        top = sbuf[slot, rs, 0:LANES] + arow[0:1, 0:LANES]
+        top = source[rs, 0:LANES] + arow[0:1, 0:LANES]
         for c in range(1, rows // LANES):
             at = slice(c * LANES, (c + 1) * LANES)
-            top = jnp.maximum(top, sbuf[slot, rs, at] + arow[0:1, at])
+            top = jnp.maximum(top, source[rs, at] + arow[0:1, at])
         top = jnp.max(top, axis=1, keepdims=True) - LIFT
         mcol[slot, rs, :] = jnp.broadcast_to(top, (quarter, LANES))
 
     def expos(k, slot, piece):
+        source = held(k, slot)
         for r in range(piece * quarter, (piece + 1) * quarter, 32):
             rs = slice(r, r + 32)
             to = slice(k * blk + r, k * blk + r + 32)
             for c in steps:
                 at = slice(c * chunk, (c + 1) * chunk)
-                e = jnp.exp2(sbuf[slot, rs, at] + (arow[0:1, at] - wide(mcol[slot, rs, :], chunk // LANES)))
+                e = jnp.exp2(source[rs, at] + (arow[0:1, at] - wide(mcol[slot, rs, :], chunk // LANES)))
                 high = e.astype(bf16)
                 low = (e - high.astype(f32)).astype(f8)
                 ehi[to, at] = high
@@ -316,7 +325,7 @@
         if pulls:
             mcol[2] = mcol[1 - slot]
         for piece in range(4):
-            if finds and piece < len(steps):
+            if finds and k + 1 >= kept and piece < len(steps):
                 scores(k + 1, 1 - slot, piece)
             if pulls:
                 products.append(pull_product(k - 1, piece))
@@ -326,7 +335,7 @@
             pull_finish(k - 1, products)
         if finds:
             for piece in range(4):
-                tops(1 - slot, piece)
+                tops(k + 1, 1 - slot, piece)
 
     def send_stats(part):
         for k in ssteps:
@@ -337,16 +346,15 @@
         return carry
 
     for piece in range(4):
-        tops(0, piece)
+        tops(0, 0, piece)
     sent, part = 1, 0
     for k in range(ns + 1):
         turn(k, k % 2, pulls=k > 0, exps=k < ns, finds=k + 1 < ns)
         if k == parts[part][1]:
             send_stats(part)
             part += 1
-            if comm:
+            if comm and part == len(parts):
                 lax.fori_loop(sent, k, send_pulled, 0)
-                sent = k
 
     for part in range(len(parts)):
         for k in ssteps:
@@ -385,7 +393,8 @@
         mass = main[2 * width : 2 * width + 1] + main[2 * width + 8 : 2 * width + 9] + rest[width : width + 1]
         return 2.0 * (xall[:, at] * mass - moved)
 
-    def push_step(k, carry):
+    def push_step(step, carry):
+        k = nt - step
         gsend[k] = push(k)
         if comm:
             gs_copy(k).start()
@@ -431,7 +440,7 @@
     dma = pltpu.SemaphoreType.DMA
     scratch = [
         ((width, rows), f32), ((ns, width, blk), f32), ((4 * width, rows), bf16), ((cols, 2 * LANES), bf16),
-        ((rows, 2 * LANES), bf16), ((rows, LANES), f8), ((2, blk, LANES), f32), ((2, blk, rows), f32),
+        ((rows, 2 * LANES), bf16), ((rows, LANES), f8), ((2, blk, LANES), f32), ((2, blk, rows), f32), ((1 + 2 * (ns // 8), blk, rows), f32),
         ((8, rows), f32), ((8, rows), f32), ((8, rows), f32), ((3, blk, LANES), f32),
         ((nt, 2, rows), f32), ((ns, 2, cols), f32), ((8, cols), f32),
         ((cols, rows), bf16), ((cols, rows), f8), ((ns, width, blk), f32),
@@ -440,7 +449,7 @@
     ]
     waits = len(column_parts(ns)) * ns
     sems = [nt, nt, 2 * ns, 2 * ns, nt, nt, waits, waits, nt, nt, ns, ns]
-    params = dict(vmem_limit_bytes=60 * 2**20, has_side_effects=True)
+    params = dict(vmem_limit_bytes=62 * 2**20, has_side_effects=True)
     if comm:
         params["collective_id"] = 0
     return pl.pallas_call(

time: 79.6 us -> 74 us (0.930)
  Pallas kernels: 78.8 us -> 73.1 us
    pallas_call x1, Pallas kernels: 77.2 us -> 71.5 us  [per_device(): run(src_points, tgt_points, log_a.reshape(1, -1), log_b.reshape(1, -1), g...]
where the time goes in v3:
time: 74 us; the launch traced here: 73.7 us
  Pallas kernels  73.1 us (99%)
    pallas_call x1, Pallas kernels, per_device(): run(src_points, tgt_points, log_a.reshape(1, -1), log_b.reshape(1, -1), g...  71.5 us
    pallas_call x1, Pallas kernels, per_device(): pl.pallas_call(hand_out, out_shape=[jax.ShapeDtypeStruct(o.shape, o.dtype...  1.57 us

profile of v3, /device:TPU:1, one launch (start us, length us, event | category | flops | bytes accessed | tf_op | source)
XLA Modules:
  0.0 73.7 jit_solution(16580898761355673377)
XLA Ops:
  0.6 71.5 %sinkhorn.1 = (f32[1,2048]{1,0:T(1,128)}, f32[1,4096]{1,0:T(1,128)}, f32[64,256]{1,0:T(8,128)}, f32[64,256]{1,0:T(8,128)}) custom-call(f32[64,256]{1,0:T(8,128)} %src_ref.1, f32[64,256]{1,0:T(8,128)} %tgt_ref.1, f32[1,2048]{1,0:T(1,128)} %bitcast.7, f32[1,4096]{1,0:T(1,128)} %bitcast.5, f32[1,4096]{1,0:T(1,128)} %bitcast.6), custom_call_target="tpu_custom_call" | custom-call | tf_op jit(solution)/shard_map/sinkhorn/pallas_call | solution.py:479
  72.1 1.6 %results.1 = (f32[1,2048]{1,0:T(1,128)}, f32[1,4096]{1,0:T(1,128)}, f32[64,256]{1,0:T(8,128)}, f32[64,256]{1,0:T(8,128)}) custom-call(f32[1,2048]{1,0:T(1,128)} %get-tuple-element.12.refs_0_, f32[1,4096]{1,0:T(1,128)} %get-tuple-element.13.refs_1_, f32[64,256]{1,0:T(8,128)} %get-tuple-element.14.refs_2_, f32[64,256]{1,0:T(8,128)} %get-tuple-element.15.refs_3_), custom_call_target="tpu_custom_call" | custom-call | tf_op jit(solution)/shard_map/results/pallas_call | solution.py:484
